TPU v7x, 512 devices: a whole 4x4x16 slice. The times are simulated.
512 devices in a mesh: dp: 64 (over z, y_lo, core), tensor: 8 (over x, y_hi).
Axes of the slice: x: 4, y: 4 (y_hi: 2, y_lo: 2; y = y_hi * 2 + y_lo), z: 16, core: 2. Of those that a mesh axis runs over, the one named last changes fastest.
Arguments:
- activations: bfloat16 [98304, 2048], P('dp', 'tensor'), may hold values from -6 to 6
- out_grads: bfloat16 [98304, 2048], P('dp', 'tensor'), may hold values from -0.001953125 to 0.001953125
- left_stat: float32 [2048, 2048], P('dp', 'tensor'), may hold values from -1 to 11, as said below
- right_stat: float32 [2048, 2048], P('dp', 'tensor'), may hold values from -1 to 11, as said below
Outputs:
- left_new: float32 [2048, 2048], P('dp', 'tensor')
- right_new: float32 [2048, 2048], P('dp', 'tensor')
- update: float32 [2048, 2048], P('dp', 'tensor')
Inputs may be any that keep to these rules, and one draw needn't show every extreme that they name: `left_stat`: symmetric, with a positive diagonal. `right_stat`: symmetric, with a positive diagonal.
All inputs are finite; a program needn't handle non-finite values.
Results may differ from a plain program's by a relative error of at most 0.0012.
Values may be sent and summed in bfloat16 or wider, within the bound.
A program may use at most 64 MiB of HBM per device.

v0:
```python
import jax
import jax.numpy as jnp
from jax import lax
from jax.sharding import Mesh
from jax.sharding import PartitionSpec as P

TENSOR = ("tensor_0", "tensor_1")
DP = ("dp_0", "dp_1", "dp_2")
DP_TENSOR = ("dp_0", "dp_1", "dp_2", "tensor_0", "tensor_1")


def in_blocks(x, dim, length):
    lengths = x.shape
    blocks = x.reshape(*lengths[:dim], length, lengths[dim] // length, *lengths[dim + 1 :])
    return jnp.moveaxis(blocks, dim, 0)


def sum_at_owner(x, axis, dim):
    length = lax.axis_size(axis)
    blocks = lax.all_to_all(in_blocks(x, dim, length), axis, 0, 0, tiled=True)
    return jnp.sum(blocks, axis=0)


def in_order(blocks, dim):
    blocks = jnp.moveaxis(blocks, 0, dim)
    lengths = blocks.shape
    return blocks.reshape(*lengths[:dim], lengths[dim] * lengths[dim + 1], *lengths[dim + 2 :])


def gather_in_order(x, axes, turns):
    blocks = x
    for k in turns:
        blocks = lax.all_gather(blocks, axes[k])
    done = turns[::-1]
    back = [done.index(k) for k in range(len(axes))]
    blocks = blocks.transpose(*back, *range(len(axes), blocks.ndim))
    return blocks.reshape(-1, *x.shape)


def gathered_by_axis(x, axes, turns, dim):
    return in_order(gather_in_order(x, axes, turns), dim)


def side_by_side(arrays, axis, dim, along):
    both = jnp.concatenate(arrays, axis=along)
    result, at, gathered = (sum_at_owner(both, axis, dim), 0, [])
    for a in arrays:
        gathered.append(lax.slice_in_dim(result, at, at + a.shape[along], axis=along))
        at += a.shape[along]
    return tuple(gathered)


def by_axis(x, axes):
    for axis in axes:
        x = lax.psum(x, axis)
    return x


def sent_to_all(x, axis):
    length = lax.axis_size(axis)
    return lax.all_to_all(jnp.broadcast_to(x[None], (length, *x.shape)), axis, 0, 0, tiled=True)


def gather_directly(x, axis, dim):
    return in_order(sent_to_all(x, axis), dim)


def local(activations, out_grads, left_stat, right_stat):
    highest = lax.Precision.HIGHEST
    tensor_count = lax.axis_size(TENSOR)
    dp_count = lax.axis_size(DP)
    col_count = out_grads.shape[1]
    full_order = col_count * tensor_count
    row_count = full_order // dp_count
    grad_terms = lax.dot_general(
        lax.all_gather(activations, TENSOR, axis=1, tiled=True),
        out_grads,
        (((0,), (0,)), ((), ())),
        preferred_element_type=jnp.float32,
    )
    grad_block = sum_at_owner(grad_terms, DP, 0)
    grad_cols = gathered_by_axis(grad_block, DP, (1, 0, 2), 0)
    left_part = lax.dot_general(
        grad_block,
        grad_cols,
        (((1,), (1,)), ((), ())),
        precision=highest,
        preferred_element_type=jnp.float32,
    )
    dp_place = lax.axis_index(DP)
    row_start = dp_place * row_count
    tensor_rows = lax.all_to_all(grad_cols, TENSOR, split_axis=0, concat_axis=1, tiled=True)
    strip_cols = lax.dynamic_slice_in_dim(tensor_rows, row_start, row_count, 1)
    right_part = lax.dot_general(
        strip_cols,
        tensor_rows,
        (((0,), (0,)), ((), ())),
        precision=highest,
        preferred_element_type=jnp.float32,
    )
    left_sum, right_sum = side_by_side((left_part, right_part), TENSOR, 1, 0)
    left_new = 0.9 * left_stat + 0.1 * left_sum
    right_new = 0.9 * right_stat + 0.1 * right_sum
    left_sq = jnp.sum(left_new * left_new)
    right_sq = jnp.sum(right_new * right_new)
    grad_sq = jnp.sum(grad_block * grad_block)
    left_total, right_total, grad_total = (
        by_axis(left_sq, DP_TENSOR),
        by_axis(right_sq, DP_TENSOR),
        by_axis(grad_sq, DP_TENSOR),
    )
    left_scale = jnp.sqrt(left_total / full_order + 1e-06)
    right_scale = jnp.sqrt(right_total / full_order + 1e-06)
    left_whole = gather_directly(left_new, TENSOR, 1)
    left_product = jnp.dot(
        left_whole, grad_cols, precision=highest, preferred_element_type=jnp.float32
    )
    pre_left = 5.0 * grad_block - left_product / left_scale
    pre_rows = gather_directly(pre_left, TENSOR, 1)
    right_product = jnp.dot(
        pre_rows,
        lax.all_gather(right_new.astype(jnp.bfloat16), DP, axis=0, tiled=True).astype(jnp.float32),
        precision=highest,
        preferred_element_type=jnp.float32,
    )
    pre_block = 5.0 * pre_left - right_product / right_scale
    pre_sq = jnp.sum(pre_block * pre_block)
    pre_total = by_axis(pre_sq, DP_TENSOR)
    factor = jnp.sqrt(grad_total + 1e-06) / jnp.sqrt(pre_total + 1e-06)
    return (left_new, right_new, pre_block * factor)


def solution(mesh):
    finer = Mesh(
        mesh.devices.reshape(16, 2, 2, 4, 2), ("dp_0", "dp_1", "dp_2", "tensor_0", "tensor_1")
    )
    placed = (P(DP, TENSOR), P(DP, TENSOR), P(DP, TENSOR), P(DP, TENSOR))
    return jax.shard_map(
        local,
        mesh=finer,
        in_specs=placed,
        out_specs=(P(DP, TENSOR), P(DP, TENSOR), P(DP, TENSOR)),
        check_vma=False,
    )
```

profile of v0, /device:TPU:16, one launch (start us, length us, event | category | flops | bytes accessed | tf_op | source)
XLA Modules:
  0.0 582.7 jit_solution(15723450914595324753)
XLA Ops:
  7.2 0.0 copy-start
  7.2 0.0 all-gather.8.cloned.1.call-start
  7.2 0.7 all-gather.8.cloned.1.call-update
  7.9 0.0 all-gather.12.cloned.1.call-start
  8.0 119.7 %all-gather.8.cloned.1.call-done = bf16[1536,2048]{1,0:T(8,128)(2,1)} async-done(((bf16[1536,256]{1,0:T(8,128)(2,1)}), bf16[1536,2048]{1,0:T(8,128)(2,1)}) %all-gather.8.cloned.1.call-update) | async-done | bytes 6291472 | tf_op jit(solution)/shard_map/all_gather | solution.py:76
  127.6 0.0 copy-done
  127.6 4.7 fusion.10
  132.4 115.6 %all_to_all.39 = f32[64,32,256]{2,1,0:T(8,128)S(1)} all-to-all(f32[64,32,256]{2,1,0:T(8,128)S(1)} %bitcast.35), channel_id=1, replica_groups=mesh['dp_0'=16,'dp_1'=2,'dp_2'=2,'tensor_0'=4,'tensor_1'=2] {'dp_0','dp_..., dimensions={0} | all-to-all | bytes 4194304 | tf_op jit(solution)/shard_map/all_to_all | solution.py:20
  248.0 0.1 reduce_sum.54
  248.1 4.7 all-gather
  252.8 0.0 all-gather.12.cloned.1.call-update
  252.8 0.0 all-gather.14.cloned.1.call-start
  252.9 61.7 %all-gather.12.cloned.1.call-done = f32[32,32,256]{2,1,0:T(8,128)} async-done(((f32[2,32,256]{2,1,0:T(8,128)}), f32[32,32,256]{2,1,0:T(8,128)}) %all-gather.12.cloned.1.call-update) | async-done | bytes 1048592 | tf_op jit(solution)/shard_map/all_gather | solution.py:33
  314.6 0.0 all-gather.14.cloned.1.call-update
  314.6 20.0 %all-gather.14.cloned.1.call-done = f32[32,2,32,256]{3,2,1,0:T(8,128)} async-done(((f32[16,2,32,256]{3,2,1,0:T(8,128)}), f32[32,2,32,256]{3,2,1,0:T(8,128)}) %all-gather.14.cloned.1.call-update) | async-done | bytes 2097168 | tf_op jit(solution)/shard_map/all_gather | solution.py:33
  334.6 3.2 copy.11
  337.8 7.2 %all-to-all-start.1 = ((f32[8,256,256]{2,1,0:T(8,128)}), f32[8,256,256]{2,1,0:T(8,128)S(1)}, u32[]{:S(2)}, u32[]{:S(2)}) async-start(f32[8,256,256]{2,1,0:T(8,128)} %bitcast.7), calls=%async_computation.1 | async-start | bytes 4194304 | tf_op jit(solution)/shard_map/all_to_all | solution.py:92
  345.0 0.0 all-gather.10.cloned.1.call-start
  345.0 3.6 fusion.11
  348.7 27.0 %all-to-all-done.1 = f32[8,256,256]{2,1,0:T(8,128)S(1)} async-done(((f32[8,256,256]{2,1,0:T(8,128)}), f32[8,256,256]{2,1,0:T(8,128)S(1)}, u32[]{:S(2)}, u32[]{:S(2)}) %all-to-all-start.1) | async-done | bytes 2097184 | tf_op jit(solution)/shard_map/all_to_all | solution.py:92
  375.6 0.0 copy-start.1
  375.6 1.3 copy-done.1
  376.9 1.9 copy.13
  378.9 2.0 fusion.4
  380.9 0.0 copy-start.4
  380.9 0.0 copy-start.5
  381.0 13.0 %all_to_all.40 = f32[8,64,256]{2,1,0:T(8,128)S(1)} all-to-all(f32[8,64,256]{2,1,0:T(8,128)S(1)} %bitcast.37), channel_id=1, replica_groups=mesh['dp_0'=16,'dp_1'=2,'dp_2'=2,'tensor_0'=4,'tensor_1'=2] {'tensor_0',..., dimensions={0} | all-to-all | bytes 1048576 | tf_op jit(solution)/shard_map/all_to_all | solution.py:20
  394.0 0.0 copy-done.4
  394.0 0.0 copy-done.5
  394.0 1.2 fusion.7
  395.2 0.0 copy-start.2
  395.2 0.0 copy-start.3
  395.2 0.0 all-gather.10.cloned.1.call-update
  395.3 0.7 broadcast_in_dim.4
  396.0 5.6 all-to-all-start.3
  401.6 0.7 multiply_reduce_fusion.2
  402.3 32.0 %all-reduce.1 = (f32[]{:T(128)}, f32[]{:T(128)}) all-reduce(f32[]{:T(128)} %get-tuple-element.27, f32[]{:T(128)} %multiply_reduce_fusion.2), channel_id=1, replica_groups=mesh['dp_0'=16,'dp_1'=2,'dp_2'=2,'tensor_0'=4,'tensor_1'=2] {'dp_0'}, use_global_device_ids=true, to_apply=%region_3.0 | all-reduce | flops 2 | bytes 16 | tf_op jit(solution)/shard_map/psum | solution.py:55
  434.3 5.6 all-reduce.9
  439.9 3.2 all-reduce.7
  443.1 11.1 %all-reduce.3 = (f32[]{:T(128)}, f32[]{:T(128)}) all-reduce(f32[]{:T(128)} %get-tuple-element.17, f32[]{:T(128)} %get-tuple-element.18), channel_id=1, replica_groups=mesh['dp_0'=16,'dp_1'=2,'dp_2'=2,'tensor_0'=4,'tensor_1'=2] {'tensor_0'}, use_global_device_ids=true, to_apply=%region_6.0 | all-reduce | flops 2 | bytes 16 | tf_op jit(solution)/shard_map/psum | solution.py:55
  454.2 7.1 %all-reduce.5 = (f32[]{:T(128)}, f32[]{:T(128)}) all-reduce(f32[]{:T(128)} %get-tuple-element.9, f32[]{:T(128)} %get-tuple-element.10), channel_id=1, replica_groups=mesh['dp_0'=16,'dp_1'=2,'dp_2'=2,'tensor_0'=4,'tensor_1'=2] {'tensor_1'}, use_global_device_ids=true, to_apply=%region_7.0 | all-reduce | flops 2 | bytes 16 | tf_op jit(solution)/shard_map/psum | solution.py:55
  462.1 0.0 all-to-all-done.3
  462.1 2.7 fusion.1
  464.8 0.7 broadcast_in_dim.5
  465.5 0.0 copy-done.2
  465.5 0.0 copy-done.3
  465.5 5.1 all-to-all-start.4
  470.6 0.6 multiply_reduce_fusion.1
  471.8 4.9 all-to-all-done.4
  476.8 38.5 %all-gather.10.cloned.1.call-done = bf16[2048,256]{1,0:T(8,128)(2,1)} async-done(((bf16[32,256]{1,0:T(8,128)(2,1)}), bf16[2048,256]{1,0:T(8,128)(2,1)}) %all-gather.10.cloned.1.call-update) | async-done | bytes 1048592 | tf_op jit(solution)/shard_map/all_gather | solution.py:122
  515.3 2.4 multiply_reduce_fusion
  517.7 29.6 %all-reduce = (f32[]{:T(128)}, f32[]{:T(128)}) all-reduce(f32[]{:T(128)} %multiply_reduce_fusion.1, f32[]{:T(128)} %get-tuple-element.29), channel_id=1, replica_groups=mesh['dp_0'=16,'dp_1'=2,'dp_2'=2,'tensor_0'=4,'tensor_1'=2] {'dp_0'}, use_global_device_ids=true, to_apply=%region_15.0 | all-reduce | flops 2 | bytes 16 | tf_op jit(solution)/shard_map/psum | solution.py:55
  547.4 5.6 all-reduce.8
  553.0 3.1 all-reduce.6
  556.1 11.2 %all-reduce.2 = (f32[]{:T(128)}, f32[]{:T(128)}) all-reduce(f32[]{:T(128)} %get-tuple-element.15, f32[]{:T(128)} %get-tuple-element.16), channel_id=1, replica_groups=mesh['dp_0'=16,'dp_1'=2,'dp_2'=2,'tensor_0'=4,'tensor_1'=2] {'tensor_0'}, use_global_device_ids=true, to_apply=%region_18.0 | all-reduce | flops 2 | bytes 16 | tf_op jit(solution)/shard_map/psum | solution.py:55
  567.2 7.1 %all-reduce.4 = (f32[]{:T(128)}, f32[]{:T(128)}) all-reduce(f32[]{:T(128)} %get-tuple-element.7, f32[]{:T(128)} %get-tuple-element.8), channel_id=1, replica_groups=mesh['dp_0'=16,'dp_1'=2,'dp_2'=2,'tensor_0'=4,'tensor_1'=2] {'tensor_1'}, use_global_device_ids=true, to_apply=%region_19.0 | all-reduce | flops 2 | bytes 16 | tf_op jit(solution)/shard_map/psum | solution.py:55
  575.6 0.6 broadcast_multiply_fusion
  (5 shorter events, 0.1 us)
Async XLA Ops:
  7.2 120.5 %copy-start = (bf16[1536,256]{1,0:T(8,128)(2,1)S(1)}, bf16[1536,256]{1,0:T(8,128)(2,1)}, u32[]{:S(2)}) copy-start(bf16[1536,256]{1,0:T(8,128)(2,1)} %param.5) | copy-start | bytes 2359300
  7.2 120.4 %all-gather.8.cloned.1.call-start = ((), (), s32[]{:S(2)}) async-start(), calls=%async_computation.5 | async-start | bytes 7077888 | tf_op jit(solution)/shard_map/all_gather | solution.py:76
  7.9 306.7 %all-gather.12.cloned.1.call-start = ((), (), s32[]{:S(2)}) async-start(), calls=%async_computation.7 | async-start | bytes 1114112 | tf_op jit(solution)/shard_map/all_gather | solution.py:33
  252.8 81.8 %all-gather.14.cloned.1.call-start = ((), (), s32[]{:S(2)}) async-start(), calls=%async_computation.8 | async-start | bytes 3145728 | tf_op jit(solution)/shard_map/all_gather | solution.py:33
  337.8 37.8 %all-to-all-start.1 = ((f32[8,256,256]{2,1,0:T(8,128)}), f32[8,256,256]{2,1,0:T(8,128)S(1)}, u32[]{:S(2)}, u32[]{:S(2)}) async-start(f32[8,256,256]{2,1,0:T(8,128)} %bitcast.7), calls=%async_computation.1 | async-start | bytes 4194304 | tf_op jit(solution)/shard_map/all_to_all | solution.py:92
  345.0 170.2 %all-gather.10.cloned.1.call-start = ((), (), s32[]{:S(2)}) async-start(), calls=%async_computation.6 | async-start | bytes 1064960 | tf_op jit(solution)/shard_map/all_gather | solution.py:122
  375.6 1.3 copy-start.1
  380.9 13.1 %copy-start.4 = (f32[32,256]{1,0:T(8,128)S(1)}, f32[32,256]{1,0:T(8,128)}, u32[]{:S(2)}) copy-start(f32[32,256]{1,0:T(8,128)} %param.7) | copy-start | bytes 98308
  380.9 13.1 %copy-start.5 = (f32[32,256]{1,0:T(8,128)S(1)}, f32[32,256]{1,0:T(8,128)}, u32[]{:S(2)}) copy-start(f32[32,256]{1,0:T(8,128)} %param.6) | copy-start | bytes 98308
  395.2 70.3 %copy-start.2 = (f32[32,256]{1,0:T(8,128)}, f32[32,256]{1,0:T(8,128)S(1)}, u32[]{:S(2)}) copy-start(f32[32,256]{1,0:T(8,128)S(1)} %get-tuple-element.28) | copy-start | bytes 98308
  395.2 70.3 %copy-start.3 = (f32[32,256]{1,0:T(8,128)}, f32[32,256]{1,0:T(8,128)S(1)}, u32[]{:S(2)}) copy-start(f32[32,256]{1,0:T(8,128)S(1)} %get-tuple-element.24) | copy-start | bytes 98308
  396.0 66.1 %all-to-all-start.3 = ((f32[8,32,256]{2,1,0:T(8,128)}), f32[8,32,256]{2,1,0:T(8,128)S(1)}, u32[]{:S(2)}, u32[]{:S(2)}) async-start(f32[8,32,256]{2,1,0:T(8,128)} %broadcast_in_dim.4), calls=%async_computation.3 | async-start | bytes 524288 | tf_op jit(solution)/shard_map/all_to_all | solution.py:61
  465.5 11.2 %all-to-all-start.4 = ((f32[8,32,256]{2,1,0:T(8,128)}), f32[8,32,256]{2,1,0:T(8,128)S(1)}, u32[]{:S(2)}, u32[]{:S(2)}) async-start(f32[8,32,256]{2,1,0:T(8,128)} %broadcast_in_dim.5), calls=%async_computation.4 | async-start | bytes 524288 | tf_op jit(solution)/shard_map/all_to_all | solution.py:61
Sparse Core Ops, SparseCore 0:
  11.1 116.5 all-gather.7
  253.0 61.5 all-gather.11
  316.7 17.9 all-gather.13
  395.4 119.8 all-gather.9
where the time goes:
time: 584 us; the launch traced here: 583 us
  waiting for transfers between devices  273 us (47%)
  blocking collectives  249 us (43%)
  starting transfers between devices  18.1 us (3%)
  between operations  16.5 us (3%)
  matrix products  15.5 us (3%)
  local copies, waits for them, and re-layouts  7.96 us (1%)
    all_to_all x2, blocking collectives, sum_at_owner(): blocks = lax.all_to_all(in_blocks(x, dim, length), axis, 0, 0, tiled=True)  129 us
    all_gather x1, waiting for transfers between devices, local(): lax.all_gather(activations, TENSOR, axis=1, tiled=True)  120 us
    psum x10, blocking collectives, by_axis(): x = lax.psum(x, axis)  116 us
    all_gather x2, waiting for transfers between devices, gather_in_order(): blocks = lax.all_gather(blocks, axes[k])  81.7 us
    all_gather x1, waiting for transfers between devices, local(): lax.all_gather(right_new.astype(jnp.bfloat16), DP, axis=0, tiled=True)  38.5 us
    all_to_all x1, waiting for transfers between devices, local(): lax.all_to_all(grad_cols, TENSOR, split_axis=0, concat_axis=1, tiled=True)  27 us
  transfers between devices with their start and end apart: 7, of which 6 were waited for; matrix products, arithmetic and copies ran while one was open for 2% of the time, Pallas kernels for 0%

commit v1 on v0

--- a/solution.py
+++ b/solution.py
@@ -73,7 +73,9 @@
     full_order = col_count * tensor_count
     row_count = full_order // dp_count
     grad_terms = lax.dot_general(
-        lax.all_gather(activations, TENSOR, axis=1, tiled=True),
+        jnp.concatenate(
+            lax.all_to_all(jnp.stack([activations] * lax.axis_size(TENSOR)), TENSOR, 0, 0), axis=1
+        ),
         out_grads,
         (((0,), (0,)), ((), ())),
         preferred_element_type=jnp.float32,

time: 584 us -> 542 us (0.928)
  the two profiles are of different devices: /device:TPU:16 before, /device:TPU:8 now
where the time goes in v1:
time: 542 us; the launch traced here: 541 us
  blocking collectives  332 us (61%)
  waiting for transfers between devices  153 us (28%)
  between operations  16.5 us (3%)
  starting transfers between devices  13.9 us (3%)
  matrix products  12.5 us (2%)
  local copies, waits for them, and re-layouts  9.96 us (2%)
    all_to_all x2, blocking collectives, sum_at_owner(): blocks = lax.all_to_all(in_blocks(x, dim, length), axis, 0, 0, tiled=True)  132 us
    psum x10, blocking collectives, by_axis(): x = lax.psum(x, axis)  116 us
    all_gather x2, waiting for transfers between devices, gather_in_order(): blocks = lax.all_gather(blocks, axes[k])  79.6 us
    all_to_all x1, blocking collectives, local(): lax.all_to_all(jnp.stack([activations] * lax.axis_size(TENSOR)), TENSOR,...  79.4 us
    all_gather x1, waiting for transfers between devices, local(): lax.all_gather(right_new.astype(jnp.bfloat16), DP, axis=0, tiled=True)  37.4 us
    all_to_all x1, waiting for transfers between devices, local(): lax.all_to_all(grad_cols, TENSOR, split_axis=0, concat_axis=1, tiled=True)  28.2 us
  transfers between devices with their start and end apart: 6, of which 5 were waited for; matrix products, arithmetic and copies ran while one was open for 2% of the time, Pallas kernels for 0%

profile of v1, /device:TPU:8, one launch (start us, length us, event | category | flops | bytes accessed | tf_op | source)
XLA Modules:
  0.0 541.0 jit_solution(11380442194920835433)
XLA Ops:
  7.2 0.0 copy-start
  7.2 0.0 all-gather.9.cloned.1.call-start
  7.2 1.5 copy.14
  8.7 0.5 stack.2
  9.2 79.4 %all_to_all.44 = bf16[8,1536,256]{1,2,0:T(8,128)(2,1)S(1)} all-to-all(bf16[8,1536,256]{1,2,0:T(8,128)(2,1)S(1)} %stack.2), channel_id=1, replica_groups=mesh['dp_0'=16,'dp_1'=2,'dp_2'=2,'tensor_0'=4,'tensor_1'=2] {'tensor_0',..., dimensions={0} | all-to-all | bytes 12582912 | tf_op jit(solution)/shard_map/all_to_all | solution.py:77
  88.7 0.0 copy-done
  88.7 1.8 fusion.2
  90.5 117.9 %all_to_all.45 = f32[64,32,256]{2,1,0:T(8,128)S(1)} all-to-all(f32[64,32,256]{2,1,0:T(8,128)S(1)} %fusion.2), channel_id=1, replica_groups=mesh['dp_0'=16,'dp_1'=2,'dp_2'=2,'tensor_0'=4,'tensor_1'=2] {'dp_0','dp_..., dimensions={0} | all-to-all | bytes 4194304 | tf_op jit(solution)/shard_map/all_to_all | solution.py:20
  208.4 0.1 reduce_sum.54
  208.5 4.7 all-gather
  213.2 0.0 all-gather.9.cloned.1.call-update
  213.3 0.0 all-gather.11.cloned.1.call-start
  213.3 59.6 %all-gather.9.cloned.1.call-done = f32[32,32,256]{2,1,0:T(8,128)} async-done(((f32[2,32,256]{2,1,0:T(8,128)}), f32[32,32,256]{2,1,0:T(8,128)}) %all-gather.9.cloned.1.call-update) | async-done | bytes 1048592 | tf_op jit(solution)/shard_map/all_gather | solution.py:33
  272.9 0.0 all-gather.11.cloned.1.call-update
  273.0 20.0 %all-gather.11.cloned.1.call-done = f32[32,2,32,256]{3,2,1,0:T(8,128)} async-done(((f32[16,2,32,256]{3,2,1,0:T(8,128)}), f32[32,2,32,256]{3,2,1,0:T(8,128)}) %all-gather.11.cloned.1.call-update) | async-done | bytes 2097168 | tf_op jit(solution)/shard_map/all_gather | solution.py:33
  293.0 3.2 copy.15
  296.2 5.8 %all-to-all-start.2 = ((f32[8,256,256]{2,1,0:T(8,128)}), f32[8,256,256]{2,1,0:T(8,128)S(1)}, u32[]{:S(2)}, u32[]{:S(2)}) async-start(f32[8,256,256]{2,1,0:T(8,128)} %bitcast.11), calls=%async_computation.2 | async-start | bytes 4194304 | tf_op jit(solution)/shard_map/all_to_all | solution.py:94
  302.0 0.0 all-gather.7.cloned.1.call-start
  302.0 3.6 fusion.12
  305.6 28.2 %all-to-all-done.2 = f32[8,256,256]{2,1,0:T(8,128)S(1)} async-done(((f32[8,256,256]{2,1,0:T(8,128)}), f32[8,256,256]{2,1,0:T(8,128)S(1)}, u32[]{:S(2)}, u32[]{:S(2)}) %all-to-all-start.2) | async-done | bytes 2097184 | tf_op jit(solution)/shard_map/all_to_all | solution.py:94
  333.9 0.0 copy-start.1
  333.9 1.3 copy-done.1
  335.1 1.9 copy.17
  337.1 2.0 fusion.6
  339.1 0.0 copy-start.4
  339.1 0.0 copy-start.5
  339.2 14.0 %all_to_all.46 = f32[8,64,256]{2,1,0:T(8,128)S(1)} all-to-all(f32[8,64,256]{2,1,0:T(8,128)S(1)} %bitcast.45), channel_id=1, replica_groups=mesh['dp_0'=16,'dp_1'=2,'dp_2'=2,'tensor_0'=4,'tensor_1'=2] {'tensor_0',..., dimensions={0} | all-to-all | bytes 1048576 | tf_op jit(solution)/shard_map/all_to_all | solution.py:20
  353.2 0.0 copy-done.4
  353.3 0.0 copy-done.5
  353.3 1.2 fusion.9
  354.5 0.0 copy-start.2
  354.5 0.0 copy-start.3
  354.5 0.0 all-gather.7.cloned.1.call-update
  354.5 0.7 broadcast_in_dim.4
  355.2 3.4 all-to-all-start.4
  358.7 0.7 multiply_reduce_fusion.2
  359.3 32.0 %all-reduce.1 = (f32[]{:T(128)}, f32[]{:T(128)}) all-reduce(f32[]{:T(128)} %get-tuple-element.27, f32[]{:T(128)} %multiply_reduce_fusion.2), channel_id=1, replica_groups=mesh['dp_0'=16,'dp_1'=2,'dp_2'=2,'tensor_0'=4,'tensor_1'=2] {'dp_0'}, use_global_device_ids=true, to_apply=%region_3.0 | all-reduce | flops 2 | bytes 16 | tf_op jit(solution)/shard_map/psum | solution.py:55
  391.3 5.6 %all-reduce.9 = (f32[]{:T(128)}, f32[]{:T(128)}) all-reduce(f32[]{:T(128)} %get-tuple-element.5, f32[]{:T(128)} %get-tuple-element.6), channel_id=1, replica_groups=mesh['dp_0'=16,'dp_1'=2,'dp_2'=2,'tensor_0'=4,'tensor_1'=2] {'dp_1'}, use_global_device_ids=true, to_apply=%region_4.0 | all-reduce | flops 2 | bytes 16 | tf_op jit(solution)/shard_map/psum | solution.py:55
  397.0 3.2 all-reduce.7
  400.1 11.5 %all-reduce.3 = (f32[]{:T(128)}, f32[]{:T(128)}) all-reduce(f32[]{:T(128)} %get-tuple-element.17, f32[]{:T(128)} %get-tuple-element.18), channel_id=1, replica_groups=mesh['dp_0'=16,'dp_1'=2,'dp_2'=2,'tensor_0'=4,'tensor_1'=2] {'tensor_0'}, use_global_device_ids=true, to_apply=%region_6.0 | all-reduce | flops 2 | bytes 16 | tf_op jit(solution)/shard_map/psum | solution.py:55
  411.7 7.1 %all-reduce.5 = (f32[]{:T(128)}, f32[]{:T(128)}) all-reduce(f32[]{:T(128)} %get-tuple-element.9, f32[]{:T(128)} %get-tuple-element.10), channel_id=1, replica_groups=mesh['dp_0'=16,'dp_1'=2,'dp_2'=2,'tensor_0'=4,'tensor_1'=2] {'tensor_1'}, use_global_device_ids=true, to_apply=%region_7.0 | all-reduce | flops 2 | bytes 16 | tf_op jit(solution)/shard_map/psum | solution.py:55
  419.6 0.0 all-to-all-done.4
  419.6 2.7 fusion.1
  422.3 0.7 broadcast_in_dim.5
  423.0 0.0 copy-done.2
  423.0 0.0 copy-done.3
  423.0 4.6 all-to-all-start.5
  427.6 0.6 multiply_reduce_fusion.1
  428.8 7.3 %all-to-all-done.5 = f32[8,32,256]{2,1,0:T(8,128)S(1)} async-done(((f32[8,32,256]{2,1,0:T(8,128)}), f32[8,32,256]{2,1,0:T(8,128)S(1)}, u32[]{:S(2)}, u32[]{:S(2)}) %all-to-all-start.5) | async-done | bytes 262176 | tf_op jit(solution)/shard_map/all_to_all | solution.py:61
  436.1 37.4 %all-gather.7.cloned.1.call-done = bf16[2048,256]{1,0:T(8,128)(2,1)} async-done(((bf16[32,256]{1,0:T(8,128)(2,1)}), bf16[2048,256]{1,0:T(8,128)(2,1)}) %all-gather.7.cloned.1.call-update) | async-done | bytes 1048592 | tf_op jit(solution)/shard_map/all_gather | solution.py:124
  473.5 2.4 multiply_reduce_fusion
  476.0 29.7 %all-reduce = (f32[]{:T(128)}, f32[]{:T(128)}) all-reduce(f32[]{:T(128)} %multiply_reduce_fusion.1, f32[]{:T(128)} %get-tuple-element.29), channel_id=1, replica_groups=mesh['dp_0'=16,'dp_1'=2,'dp_2'=2,'tensor_0'=4,'tensor_1'=2] {'dp_0'}, use_global_device_ids=true, to_apply=%region_15.0 | all-reduce | flops 2 | bytes 16 | tf_op jit(solution)/shard_map/psum | solution.py:55
  505.7 5.6 %all-reduce.8 = (f32[]{:T(128)}, f32[]{:T(128)}) all-reduce(f32[]{:T(128)} %get-tuple-element.3, f32[]{:T(128)} %get-tuple-element.4), channel_id=1, replica_groups=mesh['dp_0'=16,'dp_1'=2,'dp_2'=2,'tensor_0'=4,'tensor_1'=2] {'dp_1'}, use_global_device_ids=true, to_apply=%region_16.0 | all-reduce | flops 2 | bytes 16 | tf_op jit(solution)/shard_map/psum | solution.py:55
  511.3 3.1 all-reduce.6
  514.4 11.1 %all-reduce.2 = (f32[]{:T(128)}, f32[]{:T(128)}) all-reduce(f32[]{:T(128)} %get-tuple-element.15, f32[]{:T(128)} %get-tuple-element.16), channel_id=1, replica_groups=mesh['dp_0'=16,'dp_1'=2,'dp_2'=2,'tensor_0'=4,'tensor_1'=2] {'tensor_0'}, use_global_device_ids=true, to_apply=%region_18.0 | all-reduce | flops 2 | bytes 16 | tf_op jit(solution)/shard_map/psum | solution.py:55
  525.5 7.1 %all-reduce.4 = (f32[]{:T(128)}, f32[]{:T(128)}) all-reduce(f32[]{:T(128)} %get-tuple-element.7, f32[]{:T(128)} %get-tuple-element.8), channel_id=1, replica_groups=mesh['dp_0'=16,'dp_1'=2,'dp_2'=2,'tensor_0'=4,'tensor_1'=2] {'tensor_1'}, use_global_device_ids=true, to_apply=%region_19.0 | all-reduce | flops 2 | bytes 16 | tf_op jit(solution)/shard_map/psum | solution.py:55
  533.8 0.6 broadcast_multiply_fusion
  (5 shorter events, 0.1 us)
Async XLA Ops:
  7.2 81.5 %copy-start = (bf16[1536,256]{1,0:T(8,128)(2,1)S(1)}, bf16[1536,256]{1,0:T(8,128)(2,1)}, u32[]{:S(2)}) copy-start(bf16[1536,256]{1,0:T(8,128)(2,1)} %param.5) | copy-start | bytes 2359300
  7.2 265.7 %all-gather.9.cloned.1.call-start = ((), (), s32[]{:S(2)}) async-start(), calls=%async_computation.7 | async-start | bytes 1114112 | tf_op jit(solution)/shard_map/all_gather | solution.py:33
  213.3 79.7 %all-gather.11.cloned.1.call-start = ((), (), s32[]{:S(2)}) async-start(), calls=%async_computation.8 | async-start | bytes 3145728 | tf_op jit(solution)/shard_map/all_gather | solution.py:33
  296.2 37.7 %all-to-all-start.2 = ((f32[8,256,256]{2,1,0:T(8,128)}), f32[8,256,256]{2,1,0:T(8,128)S(1)}, u32[]{:S(2)}, u32[]{:S(2)}) async-start(f32[8,256,256]{2,1,0:T(8,128)} %bitcast.11), calls=%async_computation.2 | async-start | bytes 4194304 | tf_op jit(solution)/shard_map/all_to_all | solution.py:94
  302.0 171.6 %all-gather.7.cloned.1.call-start = ((), (), s32[]{:S(2)}) async-start(), calls=%async_computation.6 | async-start | bytes 1064960 | tf_op jit(solution)/shard_map/all_gather | solution.py:124
  333.9 1.3 copy-start.1
  339.1 14.2 %copy-start.4 = (f32[32,256]{1,0:T(8,128)S(1)}, f32[32,256]{1,0:T(8,128)}, u32[]{:S(2)}) copy-start(f32[32,256]{1,0:T(8,128)} %param.7) | copy-start | bytes 98308
  339.1 14.2 %copy-start.5 = (f32[32,256]{1,0:T(8,128)S(1)}, f32[32,256]{1,0:T(8,128)}, u32[]{:S(2)}) copy-start(f32[32,256]{1,0:T(8,128)} %param.6) | copy-start | bytes 98308
  354.5 68.5 %copy-start.2 = (f32[32,256]{1,0:T(8,128)}, f32[32,256]{1,0:T(8,128)S(1)}, u32[]{:S(2)}) copy-start(f32[32,256]{1,0:T(8,128)S(1)} %get-tuple-element.28) | copy-start | bytes 98308
  354.5 68.5 %copy-start.3 = (f32[32,256]{1,0:T(8,128)}, f32[32,256]{1,0:T(8,128)S(1)}, u32[]{:S(2)}) copy-start(f32[32,256]{1,0:T(8,128)S(1)} %get-tuple-element.24) | copy-start | bytes 98308
  355.2 64.3 %all-to-all-start.4 = ((f32[8,32,256]{2,1,0:T(8,128)}), f32[8,32,256]{2,1,0:T(8,128)S(1)}, u32[]{:S(2)}, u32[]{:S(2)}) async-start(f32[8,32,256]{2,1,0:T(8,128)} %broadcast_in_dim.4), calls=%async_computation.4 | async-start | bytes 524288 | tf_op jit(solution)/shard_map/all_to_all | solution.py:61
  423.0 13.1 %all-to-all-start.5 = ((f32[8,32,256]{2,1,0:T(8,128)}), f32[8,32,256]{2,1,0:T(8,128)S(1)}, u32[]{:S(2)}, u32[]{:S(2)}) async-start(f32[8,32,256]{2,1,0:T(8,128)} %broadcast_in_dim.5), calls=%async_computation.5 | async-start | bytes 524288 | tf_op jit(solution)/shard_map/all_to_all | solution.py:61
Sparse Core Ops, SparseCore 0:
  213.4 59.4 all-gather.8
  275.0 17.9 all-gather.10
  354.6 118.8 all-gather.6
